TPU v7x, 32 devices: a whole 2x2x4 slice. The times are simulated.
32 devices in a mesh: grp: 4 (over z), nbr: 8 (over y, x, core).
Axes of the slice: x: 2, y: 2, z: 4, core: 2. Of those that a mesh axis runs over, the one named last changes fastest.
Arguments:
- fine_coef: bfloat16 [256, 1024], P(('grp', 'nbr')), may hold values from -6 to 6
- fine_live: int32 [32], P(('grp', 'nbr')), may hold values from 2 to 8, as said below
- fine_parent: int32 [256], P(('grp', 'nbr')), may hold values from 0 to 31, as said below
- up_transfer: bfloat16 [256, 1024], P(('grp', 'nbr')), may hold values from -1 to 1
- fine_list: int32 [256, 96], P(('grp', 'nbr')), may hold values from 0 to 255, as said below
- fine_nblk: int32 [256], P(('grp', 'nbr')), may hold values from 24 to 96, as said below
- fine_blocks: bfloat16 [256, 96, 1024], P(('grp', 'nbr')), may hold values from -1 to 1
- fine_scale: float32 [256, 96], P(('grp', 'nbr')), may hold values from 0.03 to 0.3
- coarse_list: int32 [32, 96], P(('grp', 'nbr')), may hold values from 0 to 31
- coarse_nblk: int32 [32], P(('grp', 'nbr')), may hold values from 24 to 96, as said below
- coarse_blocks: bfloat16 [32, 96, 1024], P(('grp', 'nbr')), may hold values from -1 to 1
- coarse_scale: float32 [32, 96], P(('grp', 'nbr')), may hold values from 0.01 to 0.1
- down_transfer: bfloat16 [256, 1024], P(('grp', 'nbr')), may hold values from -1 to 1
Outputs:
- fine_local: bfloat16 [256, 1024], P(('grp', 'nbr'))
Inputs may be any that keep to these rules, and one draw needn't show every extreme that they name: `fine_live`: one owner in every draw holds all 8 slots. `fine_parent`: the parent of a fine slot lies in the same subtree group: slots g * 64 to (g + 1) * 64 - 1 have parents g * 8 to (g + 1) * 8 - 1. `fine_list`: every entry of a fine box's list is a live slot of the box's own subtree group. `fine_nblk`: some live box uses all 96 entries in every draw. `coarse_nblk`: some box uses all 96 entries in every draw.
All inputs are finite; a program needn't handle non-finite values.
Results may differ from a plain program's by a relative error of at most 0.0044.
Values may be sent and summed in bfloat16 or wider, within the bound.
A program may use at most 64 MiB of HBM per device.

v0:
```python
import jax
import jax.numpy as jnp
from jax import lax
from jax.sharding import PartitionSpec as P

K = 32
R = 32


def couple(blocks, scale, count, picked):
    slots = blocks.shape[0]
    width = blocks.shape[1]
    prod = jnp.einsum(
        "tjik,tjkr->tjir",
        blocks.reshape(slots, width, K, K),
        picked.reshape(slots, width, K, R),
        preferred_element_type=jnp.float32,
    )
    used = jnp.arange(width)[None, :] < count[:, None]
    weight = jnp.where(used, scale, jnp.float32(0.0))
    return jnp.sum(prod * weight[:, :, None, None], axis=1)


def body(
    fine_coef,
    fine_live,
    fine_parent,
    up_transfer,
    fine_list,
    fine_nblk,
    fine_blocks,
    fine_scale,
    coarse_list,
    coarse_nblk,
    coarse_blocks,
    coarse_scale,
    down_transfer,
):
    slots = fine_coef.shape[0]
    coarse_slots = coarse_blocks.shape[0]
    members = lax.axis_size("nbr")
    group = lax.axis_index("grp")
    live = jnp.arange(slots) < fine_live[0]
    source = jnp.where(live[:, None], fine_coef, jnp.zeros_like(fine_coef))
    group_coarse = coarse_slots * members
    local_parent = fine_parent - group * group_coarse
    lifted = jnp.einsum(
        "bij,bjr->bir",
        up_transfer.reshape(slots, K, K),
        source.reshape(slots, K, R),
        preferred_element_type=jnp.float32,
    ).reshape(slots, K * R)
    onehot = (local_parent[:, None] == jnp.arange(group_coarse)[None, :]).astype(jnp.float32)
    summed = lax.psum(
        jnp.dot(
            onehot.T, lifted, precision=lax.Precision.HIGHEST, preferred_element_type=jnp.float32
        ),
        "nbr",
    )
    everything = lax.all_gather(summed.astype(jnp.bfloat16), "grp", axis=0, tiled=True)
    group_sources = lax.all_gather(source, "nbr", axis=0, tiled=True)
    picked_coarse = everything[coarse_list]
    coarse_local = couple(coarse_blocks, coarse_scale, coarse_nblk, picked_coarse)
    coarse_local = coarse_local.reshape(coarse_slots, K * R).astype(jnp.bfloat16)
    local_source = fine_list - group * (slots * members)
    near = couple(fine_blocks, fine_scale, fine_nblk, group_sources[local_source])
    group_local = lax.all_gather(coarse_local, "nbr", axis=0, tiled=True)
    parent_rows = group_local[local_parent]
    down = jnp.einsum(
        "bij,bjr->bir",
        down_transfer.reshape(slots, K, K),
        parent_rows.reshape(slots, K, R),
        preferred_element_type=jnp.float32,
    )
    total = jnp.where(live[:, None, None], near + down, jnp.float32(0.0))
    return total.reshape(slots, K * R).astype(jnp.bfloat16)


def solution(mesh):
    placed = (
        P(("grp", "nbr"), None),
        P(("grp", "nbr")),
        P(("grp", "nbr")),
        P(("grp", "nbr"), None),
        P(("grp", "nbr"), None),
        P(("grp", "nbr")),
        P(("grp", "nbr"), None, None),
        P(("grp", "nbr"), None),
        P(("grp", "nbr"), None),
        P(("grp", "nbr")),
        P(("grp", "nbr"), None, None),
        P(("grp", "nbr"), None),
        P(("grp", "nbr"), None),
    )
    return jax.shard_map(
        body, mesh=mesh, in_specs=placed, out_specs=P(("grp", "nbr"), None), check_vma=False
    )
```

profile of v0, /device:TPU:0, one launch (start us, length us, event | category | flops | bytes accessed | tf_op | source)
XLA Modules:
  0.0 99.4 jit_solution(2779841631882370184)
XLA Ops:
  0.0 0.8 fusion.3
  1.4 0.8 broadcast_select_fusion
  2.2 10.7 %all_gather.9 = bf16[64,1024]{1,0:T(8,128)(2,1)S(1)} all-gather(bf16[8,1024]{1,0:T(8,128)(2,1)S(1)} %broadcast_select_fusion), channel_id=1, replica_groups=mesh['grp'=4,'nbr'=8] {'nbr'}, dimensions={0}, use_global_device_ids=true | all-gather | bytes 147456 | tf_op jit(solution)/shard_map/all_gather | solution.py:61
  12.9 0.7 compare_select_fusion
  13.7 2.8 %gather_fusion = bf16[768,1024]{1,0:T(8,128)(2,1)S(1)} fusion(bf16[64,1024]{1,0:T(8,128)(2,1)S(1)} %all_gather.9, s32[1024]{0:T(1024)S(1)} %pad_clamp_fusion.2), kind=kCustom, calls=%fused_computation | custom fusion | bytes 3148800 | tf_op jit(solution)/shard_map/gather | solution.py:66
  16.5 1.6 %copy.42 = bf16[768,1024]{0,1:T(8,128)(2,1)} copy(bf16[768,1024]{1,0:T(8,128)(2,1)S(1)} %gather_fusion) | data formatting | bytes 3145728 | tf_op jit(solution)/shard_map/gather | solution.py:66
  18.1 3.7 %reshape.76 = bf16[8,96,32,32]{1,0,3,2:T(8,128)(2,1)S(1)} reshape(bf16[768,1024]{0,1:T(8,128)(2,1)} %copy.42) | data formatting | bytes 3145728 | tf_op jit(solution)/shard_map/reshape | solution.py:16
  21.8 5.7 %copy.44 = bf16[8,96,32,32]{2,3,1,0:T(8,128)(2,1)} copy(bf16[8,96,32,32]{1,0,3,2:T(8,128)(2,1)S(1)} %reshape.76) | data formatting | bytes 3145728 | tf_op jit(solution)/shard_map/reshape | solution.py:16
  27.5 2.9 %copy.43 = bf16[8,96,1024]{1,2,0:T(8,128)(2,1)S(1)} copy(bf16[8,96,1024]{2,1,0:T(8,128)(2,1)} %param.19) | data formatting | bytes 3145728 | tf_op args[6]
  30.4 6.6 %copy.45 = bf16[8,96,32,32]{3,2,1,0:T(8,128)(2,1)} copy(bf16[8,96,32,32]{1,3,2,0:T(8,128)(2,1)S(1)} %bitcast.32) | data formatting | bytes 3145728 | tf_op jit(solution)/shard_map/reshape | solution.py:15
  37.1 8.1 %multiply_reduce_fusion = f32[8,32,32]{2,1,0:T(8,128)S(1)} fusion(f32[8,96]{1,0:T(8,128)S(1)} %fusion.3, bf16[8,96,32,32]{2,3,1,0:T(8,128)(2,1)} %copy.44, bf16[8,96,32,32]{3,2,1,0:T(8,128)(2,1)} %copy.45), kind=kOutput, calls=%fused_computation.3 | convolution fusion | flops 51896320 | bytes 3181568 | tf_op jit(solution)/shard_map/tjik,tjkr->tjir/dot_general | solution.py:13
  45.4 0.2 convolution_bitcast_fusion
  45.9 0.3 fusion.4
  46.1 23.6 %psum.7 = bf16[8,1024]{1,0:T(8,128)(2,1)S(1)} all-reduce(f32[8,1024]{1,0:T(8,128)S(1)} %fusion.4), channel_id=1, replica_groups=mesh['grp'=4,'nbr'=8] {'nbr'}, use_global_device_ids=true, to_apply=%region_1.2 | all-reduce | flops 8192 | bytes 49152 | tf_op jit(solution)/shard_map/psum | solution.py:54
  69.7 13.6 %all_gather.10 = bf16[32,1024]{1,0:T(8,128)(2,1)S(1)} all-gather(bf16[8,1024]{1,0:T(8,128)(2,1)S(1)} %psum.7), channel_id=1, replica_groups=mesh['grp'=4,'nbr'=8] {'grp'}, dimensions={0}, use_global_device_ids=true | all-gather | bytes 81920 | tf_op jit(solution)/shard_map/all_gather | solution.py:60
  83.3 0.8 gather_fusion.1
  84.3 1.3 %copy.50 = bf16[96,32,32]{1,2,0:T(8,128)(2,1)S(1)} copy(bf16[96,32,32]{0,2,1:T(8,128)(2,1)S(1)} %bitcast.34) | data formatting | bytes 393216 | tf_op jit(solution)/shard_map/reshape.1
  85.6 0.2 copy.49
  85.8 1.2 %copy.51 = bf16[96,32,32]{2,1,0:T(8,128)(2,1)S(1)} copy(bf16[96,32,32]{0,2,1:T(8,128)(2,1)S(1)} %bitcast.35) | data formatting | bytes 393216 | tf_op jit(solution)/shard_map/reshape
  87.7 0.5 multiply_reduce_fusion.1
  88.4 9.1 %all-gather = bf16[8,1,1024]{2,1,0:T(2,128)(2,1)S(1)} all-gather(bf16[1,1,1024]{2,1,0:T(2,128)(2,1)S(1)} %reshape.115), channel_id=1, replica_groups=mesh['grp'=4,'nbr'=8] {'nbr'}, dimensions={0}, use_global_device_ids=true | all-gather | bytes 18432 | tf_op jit(solution)/shard_map/all_gather | solution.py:67
  97.5 0.6 gather_fusion.2
  98.3 0.2 fusion.2
  98.6 0.7 convert_element_type.36
  (31 shorter events, 1.3 us)
Async XLA Ops:
  37.1 8.2 %copy-start.1 = (bf16[8,1024]{1,0:T(8,128)(2,1)S(1)}, bf16[8,1024]{1,0:T(8,128)(2,1)}, u32[]{:S(2)}) copy-start(bf16[8,1024]{1,0:T(8,128)(2,1)} %param.16) | copy-start | bytes 49156
  37.1 8.8 %copy-start.3 = (s32[8]{0:T(128)S(1)}, s32[8]{0:T(128)}, u32[]{:S(2)}) copy-start(s32[8]{0:T(128)} %param.15) | copy-start | bytes 100
  37.1 46.3 %copy-start.4 = (s32[1,96]{1,0:T(1,128)S(1)}, s32[1,96]{1,0:T(1,128)}, u32[]{:S(2)}) copy-start(s32[1,96]{1,0:T(1,128)} %param.21) | copy-start | bytes 1156
  37.1 48.5 %copy-start = (bf16[1,96,1024]{2,1,0:T(8,128)(2,1)S(1)}, bf16[1,96,1024]{2,1,0:T(8,128)(2,1)}, u32[]{:S(2)}) copy-start(bf16[1,96,1024]{2,1,0:T(8,128)(2,1)} %param.23) | copy-start | bytes 589828
  37.1 50.6 %copy-start.5 = (f32[1,96]{1,0:T(1,128)S(1)}, f32[1,96]{1,0:T(1,128)}, u32[]{:S(2)}) copy-start(f32[1,96]{1,0:T(1,128)} %param.24) | copy-start | bytes 1156
  45.2 53.0 %copy-start.2 = (bf16[8,1024]{1,0:T(8,128)(2,1)S(1)}, bf16[8,1024]{1,0:T(8,128)(2,1)}, u32[]{:S(2)}) copy-start(bf16[8,1024]{1,0:T(8,128)(2,1)} %param.25) | copy-start | bytes 49156
where the time goes:
time: 99.8 us; the launch traced here: 99.4 us
  blocking collectives  56.9 us (57%)
  local copies, waits for them, and re-layouts  29.4 us (29%)
  matrix products  9.28 us (9%)
  other arithmetic  2.28 us (2%)
  between operations  1.52 us (2%)
    psum x1, blocking collectives, body(): lax.psum(jnp.dot(onehot.T, lifted, precision=lax.Precision.HIGHEST, prefe...  23.6 us
    all_gather x1, blocking collectives, body(): lax.all_gather(summed.astype(jnp.bfloat16), 'grp', axis=0, tiled=True)  13.6 us
    all_gather x1, blocking collectives, body(): group_sources = lax.all_gather(source, 'nbr', axis=0, tiled=True)  10.7 us
    reshape x2, local copies, waits for them, and re-layouts, couple(): picked.reshape(slots, width, K, R)  9.44 us
    all_gather x1, blocking collectives, body(): group_local = lax.all_gather(coarse_local, 'nbr', axis=0, tiled=True)  9.05 us
    dot_general x2, matrix products, couple(): jnp.einsum('tjik,tjkr->tjir', blocks.reshape(slots, width, K, K), picked....  8.59 us
    reshape x1, local copies, waits for them, and re-layouts, couple(): blocks.reshape(slots, width, K, K)  6.62 us
    gather x2, local copies, waits for them, and re-layouts, body(): group_sources[local_source]  4.4 us

commit v1 on v0

v1 whole, which is shorter than its diff:
```python
import functools

import jax
import jax.numpy as jnp
from jax import lax
from jax.experimental import pallas as pl
from jax.experimental.pallas import tpu as pltpu
from jax.sharding import PartitionSpec as P

K = 32
R = 32
LANES = 128
ROWS = 8
PER = LANES // K
F32 = jnp.float32
BF16 = jnp.bfloat16
MESH = pl.DeviceIdType.MESH


def lane_group():
    return lax.broadcasted_iota(jnp.int32, (ROWS, LANES), 1) // K


def spread(tiles, scratch):
    group = lane_group()
    for q in range(ROWS):
        for m in range(PER):
            z = jnp.where(group == m, tiles[q], 0.0)
            z = z + pltpu.roll(z, K, 1)
            z = z + pltpu.roll(z, 2 * K, 1)
            scratch[pl.ds((PER * q + m) * ROWS, ROWS), :] = z
    return [scratch[pl.ds(s, K, stride=ROWS), :] for s in range(ROWS)]


def diagonal(boxes):
    group = lax.broadcasted_iota(jnp.int32, (K, LANES), 1) // K
    masks = [(group == i).astype(F32).astype(BF16) for i in range(PER)]
    rows = []
    for box in boxes:
        box = box.astype(BF16)
        rows.extend(box * mask for mask in masks)
    return jnp.concatenate(rows, axis=0)


def collect(listed, scale, count, blocks, base, sources):
    width = blocks.shape[0]
    used = lax.broadcasted_iota(jnp.int32, (1, width), 1) < count
    weight = jnp.where(used, scale, 0.0)
    high = weight.astype(BF16).astype(F32)
    low = weight - high
    hit = lax.broadcasted_iota(jnp.int32, (sources, width), 0) + base == listed
    left = jnp.concatenate(
        [jnp.where(hit, high, 0.0).astype(BF16), jnp.where(hit, low, 0.0).astype(BF16)], axis=1
    )
    right = jnp.concatenate([blocks, blocks], axis=0)
    return jnp.dot(left, right, preferred_element_type=F32)


def kernel(
    groups,
    members,
    live,
    parent,
    fnblk,
    cnblk,
    coef_h,
    up_h,
    flist_h,
    fscale_h,
    fblocks_h,
    clist_h,
    cscale_h,
    cblocks_h,
    down_h,
    out,
    coef,
    up,
    flist,
    fscale,
    fblocks,
    clist,
    cscale,
    cblocks,
    down,
    src_all,
    part,
    part_in,
    cc_all,
    cl_all,
    fine_c,
    coarse_c,
    turned_u,
    turned_d,
    turned_o,
    spread_s,
    spread_f,
    spread_c,
    spread_l,
    in_sem,
    src_send,
    src_recv,
    part_send,
    part_recv,
    cc_send,
    cc_recv,
    cl_send,
    cl_recv,
):
    ndev = groups * members
    slots = coef.shape[0]
    gbox = slots * members
    g = lax.axis_index("grp")
    n = lax.axis_index("nbr")
    me = g * members + n

    loads = [
        pltpu.make_async_copy(a, b, in_sem.at[i])
        for i, (a, b) in enumerate(
            [
                (coef_h, coef),
                (up_h, up),
                (flist_h, flist),
                (fscale_h, fscale),
                (fblocks_h, fblocks),
                (clist_h, clist),
                (cscale_h, cscale),
                (cblocks_h, cblocks),
                (down_h, down),
            ]
        )
    ]
    for load in loads:
        load.start()

    barrier = pltpu.get_barrier_semaphore()

    def everyone(act):
        def step(off, carry):
            other = lax.rem(me + off, ndev)
            act(other, (other // members, lax.rem(other, members)))
            return carry

        lax.fori_loop(1, ndev, step, 0)

    def group_of_mine(act):
        def step(off, carry):
            other = lax.rem(n + off, members)
            act(other, (g, other))
            return carry

        lax.fori_loop(1, members, step, 0)

    everyone(
        lambda other, where: pl.semaphore_signal(barrier, inc=1, device_id=where, device_id_type=MESH)
    )

    def settle(ref, count, sem):
        some = ref.at[pl.ds(0, count)]
        pltpu.make_async_copy(some, some, sem).wait()

    loads[0].wait()
    row = lax.broadcasted_iota(jnp.int32, (slots, 1), 0)
    source = jnp.where(row < live[0], coef[...].astype(F32), 0.0)
    half = source.shape[1] // 2
    src_all[n] = jnp.concatenate([source[:, :half], source[:, half:]], axis=0).astype(BF16)
    loads[1].wait()
    upf = up[...].astype(F32)
    for c in range(ROWS):
        turned_u[pl.ds(c * slots, slots), :] = upf[:, c * LANES : (c + 1) * LANES]
    own = diagonal(
        spread([source[:, q * LANES : (q + 1) * LANES] for q in range(ROWS)], spread_s)
    )
    ups = [turned_u[pl.ds(b, ROWS, stride=slots), :] for b in range(slots)]
    chunks = []
    for b in range(slots):
        mine = parent[b] - g * members
        chunks.append(
            jnp.concatenate(
                [jnp.where(mine == p, ups[b], 0.0) for p in range(members)], axis=0
            ).astype(BF16)
        )
    lifted = jnp.dot(jnp.concatenate(chunks, axis=1), own, preferred_element_type=F32)
    part[...] = lifted.reshape(members, ROWS, LANES)
    part_in[n] = part[n]

    pl.semaphore_wait(barrier, ndev - 1)

    def send_part(other, where):
        pltpu.make_async_remote_copy(
            part.at[other], part_in.at[n], part_send, part_recv, device_id=where, device_id_type=MESH
        ).start()

    def send_src(other, where):
        pltpu.make_async_remote_copy(
            src_all.at[n], src_all.at[n], src_send, src_recv, device_id=where, device_id_type=MESH
        ).start()

    group_of_mine(send_part)
    group_of_mine(send_src)

    for load in loads[5:8]:
        load.wait()
    found = collect(clist[...], cscale[...], cnblk[0], cblocks[0], 0, ndev)
    for c in range(ROWS):
        coarse_c[pl.ds(c * ndev, ndev), :] = found[:, c * LANES : (c + 1) * LANES]

    settle(part_in, members - 1, part_recv)
    coarse = part_in[0]
    for p in range(1, members):
        coarse = coarse + part_in[p]
    cc_all[me] = coarse.astype(BF16).astype(F32)

    def send_cc(other, where):
        pltpu.make_async_remote_copy(
            cc_all.at[me], cc_all.at[me], cc_send, cc_recv, device_id=where, device_id_type=MESH
        ).start()

    everyone(send_cc)

    for load in loads[2:5]:
        load.wait()
    for t in range(slots):
        found = collect(
            flist[pl.ds(t, 1), :], fscale[pl.ds(t, 1), :], fnblk[t], fblocks[t], g * gbox, gbox
        )
        for c in range(ROWS):
            fine_c[pl.ds((t * ROWS + c) * gbox, gbox), :] = found[:, c * LANES : (c + 1) * LANES]

    settle(cc_all, ndev - 1, cc_recv)

    def coarse_step(i, total):
        tiles = [cc_all[pl.ds(i * ROWS, ROWS), q, :] for q in range(ROWS)]
        right = diagonal(spread(tiles, spread_c.at[i]))
        left = jnp.concatenate(
            [coarse_c[pl.ds(i * ROWS + s, ROWS, stride=ndev), :].astype(BF16) for s in range(ROWS)],
            axis=1,
        )
        return total + jnp.dot(left, right, preferred_element_type=F32)

    local = lax.fori_loop(
        0, ndev // ROWS, coarse_step, jnp.zeros((ROWS, LANES), F32), unroll=ndev <= 32
    )
    cl_all[n] = local.astype(BF16).astype(F32)

    def send_cl(other, where):
        pltpu.make_async_remote_copy(
            cl_all.at[n], cl_all.at[n], cl_send, cl_recv, device_id=where, device_id_type=MESH
        ).start()

    group_of_mine(send_cl)

    settle(src_all, members - 1, src_recv)

    def near_step(i, total):
        block = src_all[i].astype(F32)
        tiles = [block[:ROWS, q * LANES : (q + 1) * LANES] for q in range(PER)]
        tiles += [block[ROWS:, q * LANES : (q + 1) * LANES] for q in range(PER)]
        right = diagonal(spread(tiles, spread_f.at[i]))
        left = jnp.concatenate(
            [
                fine_c[pl.ds(i * slots + s, slots * ROWS, stride=gbox), :].astype(BF16)
                for s in range(slots)
            ],
            axis=1,
        )
        return total + jnp.dot(left, right, preferred_element_type=F32)

    near = lax.fori_loop(
        0, members, near_step, jnp.zeros((slots * ROWS, LANES), F32), unroll=members <= 8
    )

    loads[8].wait()
    downf = down[...].astype(F32)
    for c in range(ROWS):
        turned_d[pl.ds(c * slots, slots), :] = downf[:, c * LANES : (c + 1) * LANES]
    downs = [turned_d[pl.ds(b, ROWS, stride=slots), :] for b in range(slots)]
    lefts = []
    for p in range(members):
        lefts.append(
            jnp.concatenate(
                [jnp.where(parent[b] - g * members == p, downs[b], 0.0) for b in range(slots)],
                axis=0,
            ).astype(BF16)
        )
    settle(cl_all, members - 1, cl_recv)
    total = near
    for i in range(members // ROWS):
        tiles = [cl_all[pl.ds(i * ROWS, ROWS), q, :] for q in range(ROWS)]
        right = diagonal(spread(tiles, spread_l.at[i]))
        left = jnp.concatenate(lefts[i * ROWS : (i + 1) * ROWS], axis=1)
        total = total + jnp.dot(left, right, preferred_element_type=F32)
    turned_o[...] = total
    keep = row < live[0]
    for c in range(ROWS):
        piece = turned_o[pl.ds(c, slots, stride=ROWS), :]
        out[:, c * LANES : (c + 1) * LANES] = jnp.where(keep, piece, 0.0).astype(BF16)

    settle(part_in, members - 1, part_send)
    settle(src_all, members - 1, src_send)
    settle(cc_all, ndev - 1, cc_send)
    settle(cl_all, members - 1, cl_send)


def body(
    fine_coef,
    fine_live,
    fine_parent,
    up_transfer,
    fine_list,
    fine_nblk,
    fine_blocks,
    fine_scale,
    coarse_list,
    coarse_nblk,
    coarse_blocks,
    coarse_scale,
    down_transfer,
):
    members = lax.axis_size("nbr")
    groups = lax.axis_size("grp")
    ndev = members * groups
    slots = fine_coef.shape[0]
    width = fine_list.shape[1]
    cwidth = coarse_list.shape[1]
    gbox = slots * members
    smem = pl.BlockSpec(memory_space=pltpu.SMEM)
    hbm = pl.BlockSpec(memory_space=pl.ANY)
    vm = pltpu.VMEM
    dma = pltpu.SemaphoreType.DMA
    flat = K * R
    return pl.pallas_call(
        functools.partial(kernel, groups, members),
        out_shape=jax.ShapeDtypeStruct((slots, flat), BF16),
        in_specs=[smem] * 4 + [hbm] * 9,
        out_specs=pl.BlockSpec(memory_space=pltpu.VMEM),
        scratch_shapes=[
            vm((slots, flat), BF16),
            vm((slots, flat), BF16),
            vm((slots, width), jnp.int32),
            vm((slots, width), F32),
            vm((slots, width, flat), BF16),
            vm((1, cwidth), jnp.int32),
            vm((1, cwidth), F32),
            vm((1, cwidth, flat), BF16),
            vm((slots, flat), BF16),
            vm((members, 2 * ROWS, flat // 2), BF16),
            vm((members, ROWS, LANES), F32),
            vm((members, ROWS, LANES), F32),
            vm((ndev, ROWS, LANES), F32),
            vm((members, ROWS, LANES), F32),
            vm((slots * ROWS * gbox, LANES), F32),
            vm((ROWS * ndev, LANES), F32),
            vm((ROWS * slots, LANES), F32),
            vm((ROWS * slots, LANES), F32),
            vm((ROWS * slots, LANES), F32),
            vm((K * ROWS, LANES), F32),
            vm((members, K * ROWS, LANES), F32),
            vm((ndev // ROWS, K * ROWS, LANES), F32),
            vm((members // ROWS, K * ROWS, LANES), F32),
            dma((9,)),
        ]
        + [dma] * 8,
        compiler_params=pltpu.CompilerParams(
            collective_id=0, has_side_effects=True, vmem_limit_bytes=40 * 1024 * 1024
        ),
    )(
        fine_live,
        fine_parent,
        fine_nblk,
        coarse_nblk,
        fine_coef,
        up_transfer,
        fine_list,
        fine_scale,
        fine_blocks,
        coarse_list,
        coarse_scale,
        coarse_blocks,
        down_transfer,
    )


def solution(mesh):
    rows = P(("grp", "nbr"), None)
    line = P(("grp", "nbr"))
    cube = P(("grp", "nbr"), None, None)
    placed = (rows, line, line, rows, rows, line, cube, rows, rows, line, cube, rows, rows)
    return jax.shard_map(body, mesh=mesh, in_specs=placed, out_specs=rows, check_vma=False)
```

time: 99.8 us -> 30.6 us (0.31)
  blocking collectives: 56.9 us -> 0 us
  local copies, waits for them, and re-layouts: 29.4 us -> 9.08 us
  Pallas kernels: 0 us -> 19.6 us
  matrix products: 9.28 us -> 0 us
  other arithmetic: 2.28 us -> 0 us
    all_gather x3 -> x0, blocking collectives: 33.3 us -> none  [the longest x1 13.6 us: body(): lax.all_gather(summed.astype(jnp.bfloat16), 'grp', axis=0, tiled=True)]
    psum x1 -> x0, blocking collectives: 23.6 us -> none  [body(): lax.psum(jnp.dot(onehot.T, lifted, precision=lax.Precision.HIGHEST, prefe...]
    pallas_call x0 -> x1, Pallas kernels: none -> 19.6 us  [body(): pl.pallas_call(functools.partial(kernel, groups, members), out_shape=jax....]
    reshape x9 -> x0, local copies, waits for them, and re-layouts: 17.8 us -> none  [the longest x2 9.44 us: couple(): picked.reshape(slots, width, K, R)]
    dot_general x5 -> x0, matrix products: 9.28 us -> none  [the longest x2 8.59 us: couple(): jnp.einsum('tjik,tjkr->tjir', blocks.reshape(slots, width, K, K), picked....]
    gather x5 -> x0, local copies, waits for them, and re-layouts: 5.92 us -> none  [the longest x2 4.4 us: body(): group_sources[local_source]]
    unnamed x16 -> x23, local copies, waits for them, and re-layouts: 3.21 us -> 9.08 us
    select_n x4 -> x0, other arithmetic: 2.25 us -> none  [the longest x1 0.79 us: body(): source = jnp.where(live[:, None], fine_coef, jnp.zeros_like(fine_coef))]
where the time goes in v1:
time: 30.6 us; the launch traced here: 30 us
  Pallas kernels  19.6 us (64%)
  local copies, waits for them, and re-layouts  9.08 us (30%)
  between operations  1.32 us (4%)
    pallas_call x1, Pallas kernels, body(): pl.pallas_call(functools.partial(kernel, groups, members), out_shape=jax....  19.6 us
    unnamed x23, local copies, waits for them, and re-layouts  9.08 us

profile of v1, /device:TPU:0, one launch (start us, length us, event | category | flops | bytes accessed | tf_op | source)
XLA Modules:
  0.0 30.0 jit_solution(8119817136976099205)
XLA Ops:
  1.3 0.0 copy-start
  1.3 1.4 %copy-done = bf16[8,96,1024]{2,1,0:T(8,128)(2,1)S(1)} copy-done((bf16[8,96,1024]{2,1,0:T(8,128)(2,1)S(1)}, bf16[8,96,1024]{2,1,0:T(8,128)(2,1)}, u32[]{:S(2)}) %copy-start) | copy-done | bytes 1572888
  2.7 0.0 copy-start.1
  2.7 0.9 %copy-done.1 = bf16[1,96,1024]{2,1,0:T(8,128)(2,1)S(1)} copy-done((bf16[1,96,1024]{2,1,0:T(8,128)(2,1)S(1)}, bf16[1,96,1024]{2,1,0:T(8,128)(2,1)}, u32[]{:S(2)}) %copy-start.1) | copy-done | bytes 196632
  3.6 0.0 copy-start.2
  3.6 0.7 %copy-done.2 = bf16[8,1024]{1,0:T(8,128)(2,1)S(1)} copy-done((bf16[8,1024]{1,0:T(8,128)(2,1)S(1)}, bf16[8,1024]{1,0:T(8,128)(2,1)}, u32[]{:S(2)}) %copy-start.2) | copy-done | bytes 16408
  4.4 0.0 copy-start.3
  4.4 0.7 %copy-done.3 = bf16[8,1024]{1,0:T(8,128)(2,1)S(1)} copy-done((bf16[8,1024]{1,0:T(8,128)(2,1)S(1)}, bf16[8,1024]{1,0:T(8,128)(2,1)}, u32[]{:S(2)}) %copy-start.3) | copy-done | bytes 16408
  5.1 0.0 copy-start.4
  5.1 0.7 %copy-done.4 = bf16[8,1024]{1,0:T(8,128)(2,1)S(1)} copy-done((bf16[8,1024]{1,0:T(8,128)(2,1)S(1)}, bf16[8,1024]{1,0:T(8,128)(2,1)}, u32[]{:S(2)}) %copy-start.4) | copy-done | bytes 16408
  5.8 0.0 copy-start.5
  5.8 0.7 %copy-done.5 = s32[8,96]{1,0:T(8,128)S(1)} copy-done((s32[8,96]{1,0:T(8,128)S(1)}, s32[8,96]{1,0:T(8,128)}, u32[]{:S(2)}) %copy-start.5) | copy-done | bytes 3096
  6.5 0.0 copy-start.6
  6.5 0.7 %copy-done.6 = f32[8,96]{1,0:T(8,128)S(1)} copy-done((f32[8,96]{1,0:T(8,128)S(1)}, f32[8,96]{1,0:T(8,128)}, u32[]{:S(2)}) %copy-start.6) | copy-done | bytes 3096
  7.2 0.0 copy-start.7
  7.2 0.7 %copy-done.7 = s32[8]{0:T(128)S(1)} copy-done((s32[8]{0:T(128)S(1)}, s32[8]{0:T(128)}, u32[]{:S(2)}) %copy-start.7) | copy-done | bytes 56
  7.8 0.0 copy-start.8
  7.8 0.7 %copy-done.8 = s32[8]{0:T(128)S(1)} copy-done((s32[8]{0:T(128)S(1)}, s32[8]{0:T(128)}, u32[]{:S(2)}) %copy-start.8) | copy-done | bytes 56
  8.5 0.0 copy-start.9
  8.5 0.7 %copy-done.9 = s32[1,96]{1,0:T(1,128)S(1)} copy-done((s32[1,96]{1,0:T(1,128)S(1)}, s32[1,96]{1,0:T(1,128)}, u32[]{:S(2)}) %copy-start.9) | copy-done | bytes 408
  9.1 0.0 copy-start.10
  9.1 0.7 %copy-done.10 = f32[1,96]{1,0:T(1,128)S(1)} copy-done((f32[1,96]{1,0:T(1,128)S(1)}, f32[1,96]{1,0:T(1,128)}, u32[]{:S(2)}) %copy-start.10) | copy-done | bytes 408
  9.8 19.6 %shard_map.127 = bf16[8,1024]{1,0:T(8,128)(2,1)S(1)} custom-call(s32[1]{0:T(128)S(6)} %copy.15.live, s32[8]{0:T(128)S(1)} %copy-done.7, s32[8]{0:T(128)S(1)} %copy-done.8, s32[1]{0:T(128)S(6)} %copy.16.cnblk, bf16[8,1024]{1,0:T(8,128)(2,1)S(1)} %copy-done.2, bf16[8,1024]{1,0:T(8,128)(2,1)S(1)} %copy-done.3, s32[8,96]{1,0:T(8,128)S(1)} %copy-done.5, ...), custom_call_target="tpu_custom_call" | custom-call | tf_op jit(solution)/shard_map/pallas_call | solution.py:331
  29.4 0.6 %copy.17 = bf16[8,1024]{1,0:T(8,128)(2,1)} copy(bf16[8,1024]{1,0:T(8,128)(2,1)S(1)} %shard_map.127) | data formatting | bytes 32768
Async XLA Ops:
  1.3 1.4 %copy-start = (bf16[8,96,1024]{2,1,0:T(8,128)(2,1)S(1)}, bf16[8,96,1024]{2,1,0:T(8,128)(2,1)}, u32[]{:S(2)}) copy-start(bf16[8,96,1024]{2,1,0:T(8,128)(2,1)} %fblocks_h.1) | copy-start | bytes 4718596
  2.7 0.9 %copy-start.1 = (bf16[1,96,1024]{2,1,0:T(8,128)(2,1)S(1)}, bf16[1,96,1024]{2,1,0:T(8,128)(2,1)}, u32[]{:S(2)}) copy-start(bf16[1,96,1024]{2,1,0:T(8,128)(2,1)} %cblocks_h.1) | copy-start | bytes 589828
  3.6 0.7 %copy-start.2 = (bf16[8,1024]{1,0:T(8,128)(2,1)S(1)}, bf16[8,1024]{1,0:T(8,128)(2,1)}, u32[]{:S(2)}) copy-start(bf16[8,1024]{1,0:T(8,128)(2,1)} %coef_h.1) | copy-start | bytes 49156
  4.4 0.7 %copy-start.3 = (bf16[8,1024]{1,0:T(8,128)(2,1)S(1)}, bf16[8,1024]{1,0:T(8,128)(2,1)}, u32[]{:S(2)}) copy-start(bf16[8,1024]{1,0:T(8,128)(2,1)} %up_h.1) | copy-start | bytes 49156
  5.1 0.7 %copy-start.4 = (bf16[8,1024]{1,0:T(8,128)(2,1)S(1)}, bf16[8,1024]{1,0:T(8,128)(2,1)}, u32[]{:S(2)}) copy-start(bf16[8,1024]{1,0:T(8,128)(2,1)} %down_h.1) | copy-start | bytes 49156
  5.8 0.7 %copy-start.5 = (s32[8,96]{1,0:T(8,128)S(1)}, s32[8,96]{1,0:T(8,128)}, u32[]{:S(2)}) copy-start(s32[8,96]{1,0:T(8,128)} %flist_h.1) | copy-start | bytes 9220
  6.5 0.7 %copy-start.6 = (f32[8,96]{1,0:T(8,128)S(1)}, f32[8,96]{1,0:T(8,128)}, u32[]{:S(2)}) copy-start(f32[8,96]{1,0:T(8,128)} %fscale_h.1) | copy-start | bytes 9220
  7.2 0.7 %copy-start.7 = (s32[8]{0:T(128)S(1)}, s32[8]{0:T(128)}, u32[]{:S(2)}) copy-start(s32[8]{0:T(128)} %parent.1) | copy-start | bytes 100
  7.8 0.7 %copy-start.8 = (s32[8]{0:T(128)S(1)}, s32[8]{0:T(128)}, u32[]{:S(2)}) copy-start(s32[8]{0:T(128)} %fnblk.1) | copy-start | bytes 100
  8.5 0.7 %copy-start.9 = (s32[1,96]{1,0:T(1,128)S(1)}, s32[1,96]{1,0:T(1,128)}, u32[]{:S(2)}) copy-start(s32[1,96]{1,0:T(1,128)} %clist_h.1) | copy-start | bytes 1156
  9.1 0.7 %copy-start.10 = (f32[1,96]{1,0:T(1,128)S(1)}, f32[1,96]{1,0:T(1,128)}, u32[]{:S(2)}) copy-start(f32[1,96]{1,0:T(1,128)} %cscale_h.1) | copy-start | bytes 1156

commit v2 on v1

--- a/solution.py
+++ b/solution.py
@@ -59,10 +59,10 @@
 def kernel(
     groups,
     members,
-    live,
-    parent,
-    fnblk,
-    cnblk,
+    live_h,
+    parent_h,
+    fnblk_h,
+    cnblk_h,
     coef_h,
     up_h,
     flist_h,
@@ -73,6 +73,10 @@
     cblocks_h,
     down_h,
     out,
+    live,
+    parent,
+    fnblk,
+    cnblk,
     coef,
     up,
     flist,
@@ -86,6 +90,7 @@
     part,
     part_in,
     cc_all,
+    cc_wide,
     cl_all,
     fine_c,
     coarse_c,
@@ -113,6 +118,37 @@
     n = lax.axis_index("nbr")
     me = g * members + n
 
+    rank = [n] + [lax.rem(n + off, members) for off in range(1, members)]
+
+    def columns(act):
+        def step(off, carry):
+            other = lax.rem(g + off, groups)
+            act(other * members + n, (other, n))
+            return carry
+
+        lax.fori_loop(1, groups, step, 0, unroll=groups <= 4)
+
+    def other_groups(act):
+        def step(off, carry):
+            other = lax.rem(g + off, groups)
+            for m in range(members):
+                act(other * members + rank[m], (other, rank[m]))
+            return carry
+
+        lax.fori_loop(1, groups, step, 0, unroll=groups <= 4)
+
+    def group_of_mine(act):
+        for off in range(1, members):
+            act(rank[off], (g, rank[off]))
+
+    barrier = pltpu.get_barrier_semaphore()
+
+    def greet(other, where):
+        pl.semaphore_signal(barrier, inc=1, device_id=where, device_id_type=MESH)
+
+    group_of_mine(greet)
+    columns(greet)
+
     loads = [
         pltpu.make_async_copy(a, b, in_sem.at[i])
         for i, (a, b) in enumerate(
@@ -126,38 +162,22 @@
                 (cscale_h, cscale),
                 (cblocks_h, cblocks),
                 (down_h, down),
+                (live_h, live),
+                (parent_h, parent),
+                (fnblk_h, fnblk),
+                (cnblk_h, cnblk),
             ]
         )
     ]
     for load in loads:
         load.start()
 
-    barrier = pltpu.get_barrier_semaphore()
-
-    def everyone(act):
-        def step(off, carry):
-            other = lax.rem(me + off, ndev)
-            act(other, (other // members, lax.rem(other, members)))
-            return carry
-
-        lax.fori_loop(1, ndev, step, 0)
-
-    def group_of_mine(act):
-        def step(off, carry):
-            other = lax.rem(n + off, members)
-            act(other, (g, other))
-            return carry
-
-        lax.fori_loop(1, members, step, 0)
-
-    everyone(
-        lambda other, where: pl.semaphore_signal(barrier, inc=1, device_id=where, device_id_type=MESH)
-    )
-
     def settle(ref, count, sem):
         some = ref.at[pl.ds(0, count)]
         pltpu.make_async_copy(some, some, sem).wait()
 
+    for load in loads[9:]:
+        load.wait()
     loads[0].wait()
     row = lax.broadcasted_iota(jnp.int32, (slots, 1), 0)
     source = jnp.where(row < live[0], coef[...].astype(F32), 0.0)
@@ -183,7 +203,7 @@
     part[...] = lifted.reshape(members, ROWS, LANES)
     part_in[n] = part[n]
 
-    pl.semaphore_wait(barrier, ndev - 1)
+    pl.semaphore_wait(barrier, members + groups - 2)
 
     def send_part(other, where):
         pltpu.make_async_remote_copy(
@@ -208,14 +228,15 @@
     coarse = part_in[0]
     for p in range(1, members):
         coarse = coarse + part_in[p]
-    cc_all[me] = coarse.astype(BF16).astype(F32)
+    cc_all[me] = coarse.astype(BF16)
 
     def send_cc(other, where):
         pltpu.make_async_remote_copy(
             cc_all.at[me], cc_all.at[me], cc_send, cc_recv, device_id=where, device_id_type=MESH
         ).start()
 
-    everyone(send_cc)
+    other_groups(send_cc)
+    group_of_mine(send_cc)
 
     for load in loads[2:5]:
         load.wait()
@@ -229,7 +250,8 @@
     settle(cc_all, ndev - 1, cc_recv)
 
     def coarse_step(i, total):
-        tiles = [cc_all[pl.ds(i * ROWS, ROWS), q, :] for q in range(ROWS)]
+        cc_wide[pl.ds(i * ROWS, ROWS)] = cc_all[pl.ds(i * ROWS, ROWS)].astype(F32)
+        tiles = [cc_wide[pl.ds(i * ROWS, ROWS), q, :] for q in range(ROWS)]
         right = diagonal(spread(tiles, spread_c.at[i]))
         left = jnp.concatenate(
             [coarse_c[pl.ds(i * ROWS + s, ROWS, stride=ndev), :].astype(BF16) for s in range(ROWS)],
@@ -323,17 +345,20 @@
     width = fine_list.shape[1]
     cwidth = coarse_list.shape[1]
     gbox = slots * members
-    smem = pl.BlockSpec(memory_space=pltpu.SMEM)
-    hbm = pl.BlockSpec(memory_space=pl.ANY)
+    hbm = pl.BlockSpec(memory_space=pltpu.HBM)
     vm = pltpu.VMEM
     dma = pltpu.SemaphoreType.DMA
     flat = K * R
     return pl.pallas_call(
         functools.partial(kernel, groups, members),
-        out_shape=jax.ShapeDtypeStruct((slots, flat), BF16),
-        in_specs=[smem] * 4 + [hbm] * 9,
+        out_shape=pltpu.VMEM((slots, flat), BF16),
+        in_specs=[hbm] * 13,
         out_specs=pl.BlockSpec(memory_space=pltpu.VMEM),
         scratch_shapes=[
+            pltpu.SMEM((1,), jnp.int32),
+            pltpu.SMEM((slots,), jnp.int32),
+            pltpu.SMEM((slots,), jnp.int32),
+            pltpu.SMEM((1,), jnp.int32),
             vm((slots, flat), BF16),
             vm((slots, flat), BF16),
             vm((slots, width), jnp.int32),
@@ -346,6 +371,7 @@
             vm((members, 2 * ROWS, flat // 2), BF16),
             vm((members, ROWS, LANES), F32),
             vm((members, ROWS, LANES), F32),
+            vm((ndev, ROWS, LANES), BF16),
             vm((ndev, ROWS, LANES), F32),
             vm((members, ROWS, LANES), F32),
             vm((slots * ROWS * gbox, LANES), F32),
@@ -357,11 +383,11 @@
             vm((members, K * ROWS, LANES), F32),
             vm((ndev // ROWS, K * ROWS, LANES), F32),
             vm((members // ROWS, K * ROWS, LANES), F32),
-            dma((9,)),
+            dma((13,)),
         ]
         + [dma] * 8,
         compiler_params=pltpu.CompilerParams(
-            collective_id=0, has_side_effects=True, vmem_limit_bytes=40 * 1024 * 1024
+            collective_id=0, has_side_effects=True, vmem_limit_bytes=60 * 1024 * 1024
         ),
     )(
         fine_live,

time: 30.6 us -> 19.3 us (0.63); the launches traced: 30 us -> 19.1 us
  local copies, waits for them, and re-layouts: 9.08 us -> 0.61 us
  Pallas kernels: 19.6 us -> 17.2 us
    unnamed x23 -> x1, local copies, waits for them, and re-layouts: 9.08 us -> 0.61 us
    pallas_call x1, Pallas kernels: 19.6 us -> 17.2 us  [body(): pl.pallas_call(functools.partial(kernel, groups, members), out_shape=pltp...]
where the time goes in v2:
time: 19.3 us; the launch traced here: 19.1 us
  Pallas kernels  17.2 us (89%)
  between operations  1.3 us (7%)
  local copies, waits for them, and re-layouts  0.61 us (3%)
    pallas_call x1, Pallas kernels, body(): pl.pallas_call(functools.partial(kernel, groups, members), out_shape=pltp...  17.2 us
    unnamed x1, local copies, waits for them, and re-layouts  0.61 us

profile of v2, /device:TPU:0, one launch (start us, length us, event | category | flops | bytes accessed | tf_op | source)
XLA Modules:
  0.0 19.1 jit_solution(5523952109360482132)
XLA Ops:
  1.3 17.2 %shard_map.127 = bf16[8,1024]{1,0:T(8,128)(2,1)S(1)} custom-call(s32[1]{0:T(128)S(6)} %copy.16.live_h, s32[8]{0:T(128)} %parent_h.1, s32[8]{0:T(128)} %fnblk_h.1, s32[1]{0:T(128)S(6)} %copy.17.cnblk_h, bf16[8,1024]{1,0:T(8,128)(2,1)} %coef_h.1, bf16[8,1024]{1,0:T(8,128)(2,1)} %up_h.1, s32[8,96]{1,0:T(8,128)} %flist_h.1, f32[8,96]{1,0:T(8,128)} %fscale_h.1, ...), custom_call_target="tpu_custom_call" | custom-call | tf_op jit(solution)/shard_map/pallas_call | solution.py:352
  18.5 0.6 %copy.15 = bf16[8,1024]{1,0:T(8,128)(2,1)} copy(bf16[8,1024]{1,0:T(8,128)(2,1)S(1)} %shard_map.127) | data formatting | bytes 32768

commit v3 on v2

--- a/solution.py
+++ b/solution.py
@@ -141,14 +141,6 @@
         for off in range(1, members):
             act(rank[off], (g, rank[off]))
 
-    barrier = pltpu.get_barrier_semaphore()
-
-    def greet(other, where):
-        pl.semaphore_signal(barrier, inc=1, device_id=where, device_id_type=MESH)
-
-    group_of_mine(greet)
-    columns(greet)
-
     loads = [
         pltpu.make_async_copy(a, b, in_sem.at[i])
         for i, (a, b) in enumerate(
@@ -169,21 +161,31 @@
             ]
         )
     ]
-    for load in loads:
+    first = [loads[i] for i in (9, 10, 0, 1)]
+    for load in first:
         load.start()
+
+    barrier = pltpu.get_barrier_semaphore()
+
+    def greet(other, where):
+        pl.semaphore_signal(barrier, inc=1, device_id=where, device_id_type=MESH)
+
+    group_of_mine(greet)
+    columns(greet)
+
 
     def settle(ref, count, sem):
         some = ref.at[pl.ds(0, count)]
         pltpu.make_async_copy(some, some, sem).wait()
 
-    for load in loads[9:]:
-        load.wait()
+    loads[9].wait()
     loads[0].wait()
     row = lax.broadcasted_iota(jnp.int32, (slots, 1), 0)
     source = jnp.where(row < live[0], coef[...].astype(F32), 0.0)
     half = source.shape[1] // 2
     src_all[n] = jnp.concatenate([source[:, :half], source[:, half:]], axis=0).astype(BF16)
     loads[1].wait()
+    loads[10].wait()
     upf = up[...].astype(F32)
     for c in range(ROWS):
         turned_u[pl.ds(c * slots, slots), :] = upf[:, c * LANES : (c + 1) * LANES]
@@ -217,9 +219,11 @@
 
     group_of_mine(send_part)
     group_of_mine(send_src)
-
-    for load in loads[5:8]:
-        load.wait()
+    for i in (5, 6, 7, 12, 2, 3, 11, 4, 8):
+        loads[i].start()
+
+    for i in (5, 6, 7, 12):
+        loads[i].wait()
     found = collect(clist[...], cscale[...], cnblk[0], cblocks[0], 0, ndev)
     for c in range(ROWS):
         coarse_c[pl.ds(c * ndev, ndev), :] = found[:, c * LANES : (c + 1) * LANES]
@@ -238,8 +242,8 @@
     other_groups(send_cc)
     group_of_mine(send_cc)
 
-    for load in loads[2:5]:
-        load.wait()
+    for i in (2, 3, 11, 4):
+        loads[i].wait()
     for t in range(slots):
         found = collect(
             flist[pl.ds(t, 1), :], fscale[pl.ds(t, 1), :], fnblk[t], fblocks[t], g * gbox, gbox

time: 19.3 us -> 19.2 us (level)
  Pallas kernels: 17.2 us -> 17 us
where the time goes in v3:
time: 19.2 us; the launch traced here: 18.9 us
  Pallas kernels  17 us (89%)
  between operations  1.3 us (7%)
  local copies, waits for them, and re-layouts  0.61 us (3%)
    pallas_call x1, Pallas kernels, body(): pl.pallas_call(functools.partial(kernel, groups, members), out_shape=pltp...  17 us
    unnamed x1, local copies, waits for them, and re-layouts  0.61 us

profile of v3, /device:TPU:0, one launch (start us, length us, event | category | flops | bytes accessed | tf_op | source)
XLA Modules:
  0.0 18.9 jit_solution(2867807326080092960)
XLA Ops:
  1.3 17.0 %shard_map.127 = bf16[8,1024]{1,0:T(8,128)(2,1)S(1)} custom-call(s32[1]{0:T(128)S(6)} %copy.16.live_h, s32[8]{0:T(128)} %parent_h.1, s32[8]{0:T(128)} %fnblk_h.1, s32[1]{0:T(128)S(6)} %copy.17.cnblk_h, bf16[8,1024]{1,0:T(8,128)(2,1)} %coef_h.1, bf16[8,1024]{1,0:T(8,128)(2,1)} %up_h.1, s32[8,96]{1,0:T(8,128)} %flist_h.1, f32[8,96]{1,0:T(8,128)} %fscale_h.1, ...), custom_call_target="tpu_custom_call" | custom-call | tf_op jit(solution)/shard_map/pallas_call | solution.py:356
  18.3 0.6 %copy.15 = bf16[8,1024]{1,0:T(8,128)(2,1)} copy(bf16[8,1024]{1,0:T(8,128)(2,1)S(1)} %shard_map.127) | data formatting | bytes 32768
